TPU v7x, 256 devices: a whole 4x4x8 slice. The times are simulated.
256 devices in a mesh: dev: 256 (over x, y, z, core).
Axes of the slice: x: 4, y: 4, z: 8, core: 2. Of those that a mesh axis runs over, the one named last changes fastest.
Arguments:
- features: bfloat16 [262144, 768], P('dev'), may hold values from -6 to 6
- eigvecs: bfloat16 [262144, 64], P('dev'), may hold values from -5 to 5
Outputs:
- updated: float32 [262144, 64], P('dev')
All inputs are finite; a program needn't handle non-finite values.
Results may differ from a plain program's by a relative error of at most 0.039.
Values may be sent and summed in bfloat16 or wider, within the bound.
A program may use at most 64 MiB of HBM per device.

v0:
```python
import math

import jax
import jax.numpy as jnp
from jax import lax
from jax.sharding import PartitionSpec as P

ROUNDS = 3


def shifted(value, axis, steps):
    count = lax.axis_size(axis)
    pairs = [(source, (source + steps) % count) for source in range(count)]
    return lax.ppermute(value, axis, pairs)


def normalize(features):
    values = features.astype(jnp.float32)
    unit = values * lax.rsqrt(jnp.mean(values * values, axis=-1, keepdims=True) + 1e-06)
    return unit.astype(jnp.bfloat16)


def squares(unit):
    values = unit.astype(jnp.float32)
    return jnp.sum(values * values, axis=-1)


def affinity(rows_unit, rows_sq, cols_unit, cols_sq):
    width = rows_unit.shape[1]
    kappa = math.sqrt(2.0 * width)
    inner = lax.dot_general(
        rows_unit, cols_unit, (((1,), (1,)), ((), ())), preferred_element_type=jnp.float32
    )
    return jnp.exp(kappa * (inner - 0.5 * (rows_sq[:, None] + cols_sq[None, :])) / width)


def zero_diagonal(kernel):
    size = kernel.shape[0]
    index = lax.broadcasted_iota(jnp.int32, (size, size), 0)
    other = lax.broadcasted_iota(jnp.int32, (size, size), 1)
    return jnp.where(index == other, jnp.zeros_like(kernel), kernel)


def shards(features, eigvecs):
    tiles = features.shape[0]
    width = features.shape[1]
    unit = normalize(features)
    sqnorm = squares(unit)
    own = zero_diagonal(affinity(unit, sqnorm, unit, sqnorm))
    degree = jnp.sum(own, axis=1)
    stored_low = []
    for step in range(1, ROUNDS + 1):
        lower = shifted(unit, "dev", step)
        low_kernel = affinity(unit, sqnorm, lower, squares(lower))
        degree = degree + jnp.sum(low_kernel, axis=1)
        stored_low.append(low_kernel.astype(jnp.bfloat16))
        degree = degree + shifted(jnp.sum(low_kernel, axis=0), "dev", -step)
    inverse = lax.rsqrt(degree)
    scaled = (eigvecs.astype(jnp.float32) * inverse[:, None]).astype(jnp.bfloat16)
    total = jnp.dot(own.astype(jnp.bfloat16), scaled, preferred_element_type=jnp.float32)
    packed = jnp.concatenate([unit, scaled], axis=1)
    for step in range(1, ROUNDS + 1):
        arrived = shifted(packed, "dev", step)
        lower = arrived[:, :width]
        lower_scaled = arrived[:, width:]
        low_kernel = affinity(unit, sqnorm, lower, squares(lower)).astype(jnp.bfloat16)
        total = total + jnp.dot(low_kernel, lower_scaled, preferred_element_type=jnp.float32)
        returned = lax.dot_general(
            low_kernel, scaled, (((0,), (0,)), ((), ())), preferred_element_type=jnp.float32
        )
        total = total + shifted(returned.astype(jnp.bfloat16), "dev", -step).astype(returned.dtype)
    factor = 0.25 * math.sqrt((2 * ROUNDS + 1) * tiles)
    return factor * inverse[:, None] * total


def solution(mesh):
    return jax.shard_map(
        shards,
        mesh=mesh,
        in_specs=(P("dev", None), P("dev", None)),
        out_specs=P("dev", None),
        check_vma=False,
    )
```

profile of v0, /device:TPU:1, one launch (start us, length us, event | category | flops | bytes accessed | tf_op | source)
XLA Modules:
  0.0 252.7 jit_solution(10146943808760458090)
XLA Ops:
  0.0 1.7 copy.10
  2.1 0.5 multiply_reduce_fusion.6
  2.6 4.5 %collective-permute-start.4 = (bf16[1024,768]{0,1:T(8,128)(2,1)S(1)}, bf16[1024,768]{0,1:T(8,128)(2,1)S(1)}, u32[]{:S(2)}, u32[]{:S(2)}) collective-permute-start(bf16[1024,768]{0,1:T(8,128)(2,1)S(1)} %get-tuple-element.19), channel_id=1, source_target_pairs={{0,3},{1,4},{2,5},{3,6},{4,7},{5,8},{6,9},{7,10},{8,11},{9,12},{10... | collective-permute-start | bytes 4718600 | tf_op jit(solution)/shard_map/ppermute | solution.py:14
  7.1 1.6 collective-permute-start.2
  9.0 1.9 fusion.29
  10.9 54.9 %collective-permute-done.4 = bf16[1024,768]{0,1:T(8,128)(2,1)S(1)} collective-permute-done((bf16[1024,768]{0,1:T(8,128)(2,1)S(1)}, bf16[1024,768]{0,1:T(8,128)(2,1)S(1)}, u32[]{:S(2)}, u32[]{:S(2)}) %collective-permute-start.4) | collective-permute-done | bytes 1572896 | tf_op jit(solution)/shard_map/ppermute | solution.py:14
  66.1 32.6 %collective-permute-done.2 = bf16[1024,768]{0,1:T(8,128)(2,1)S(1)} collective-permute-done((bf16[1024,768]{0,1:T(8,128)(2,1)S(1)}, bf16[1024,768]{0,1:T(8,128)(2,1)S(1)}, u32[]{:S(2)}, u32[]{:S(2)}) %collective-permute-start.2) | collective-permute-done | bytes 1572896 | tf_op jit(solution)/shard_map/ppermute | solution.py:14
  99.1 1.9 fusion.30
  101.0 1.9 fusion.31
  102.8 4.9 %collective-permute-done = bf16[1024,768]{0,1:T(8,128)(2,1)S(1)} collective-permute-done((bf16[1024,768]{0,1:T(8,128)(2,1)S(1)}, bf16[1024,768]{0,1:T(8,128)(2,1)S(1)}, u32[]{:S(2)}, u32[]{:S(2)}) %collective-permute-start) | collective-permute-done | bytes 1572896 | tf_op jit(solution)/shard_map/ppermute | solution.py:14
  108.1 6.9 %fusion.3 = (f32[1024]{0:T(1024)S(1)}, f32[1024]{0:T(1024)S(1)}, f32[1024]{0:T(1024)S(1)}, f32[1024]{0:T(1024)S(1)}, f32[1024]{0:T(1024)S(1)}, /*index=5*/f32[1024]{0:T(1024)S(1)}, f32[1024]{0:T(1024)S(1)}) fusion(f32[1024]{0:T(1024)S(1)} %multiply_reduce_fusion.5, f32[1024]{0:T(1024)S(1)} %get-tuple-element.18, f32[1024,1024]{0,1:T(8,128)S(1)} %fusion.30, ...), kind=kOutput, calls=%fused_computation.20 | convolution fusion | flops 1636819968 | bytes 15773696 | tf_op jit(solution)/shard_map/dot_general | solution.py:31
  115.0 9.0 %collective-permute-start.1 = (f32[1024]{0:T(1024)S(1)}, f32[1024]{0:T(1024)S(1)}, u32[]{:S(2)}, u32[]{:S(2)}) collective-permute-start(f32[1024]{0:T(1024)S(1)} %get-tuple-element.6), channel_id=1, source_target_pairs={{0,255},{1,0},{2,1},{3,2},{4,3},{5,4},{6,5},{7,6},{8,7},{9,8},{10,... | collective-permute-start | bytes 12296 | tf_op jit(solution)/shard_map/ppermute | solution.py:14
  124.0 0.8 collective-permute-start.3
  124.8 2.2 collective-permute-start.5
  127.0 1.7 collective-permute-done.5
  128.9 0.9 collective-permute-start.6
  130.1 1.2 fusion.10
  131.3 34.8 %collective-permute-done.6 = bf16[1024,832]{0,1:T(8,128)(2,1)S(1)} collective-permute-done((bf16[1024,832]{0,1:T(8,128)(2,1)S(1)}, bf16[1024,832]{0,1:T(8,128)(2,1)S(1)}, u32[]{:S(2)}, u32[]{:S(2)}) %collective-permute-start.6) | collective-permute-done | bytes 1703968 | tf_op jit(solution)/shard_map/ppermute | solution.py:14
  166.4 2.4 exponential_convert_fusion.2
  168.9 0.8 convolution_convert_fusion.2
  169.6 8.2 %collective-permute-start.7 = (bf16[1024,64]{0,1:T(8,128)(2,1)S(1)}, bf16[1024,64]{0,1:T(8,128)(2,1)S(1)}, u32[]{:S(2)}, u32[]{:S(2)}) collective-permute-start(bf16[1024,64]{0,1:T(8,128)(2,1)S(1)} %convolution_convert_fusion.2), channel_id=1, source_target_pairs={{0,255},{1,0},{2,1},{3,2},{4,3},{5,4},{6,5},{7,6},{8,7},{9,8},{10,... | collective-permute-start | bytes 393224 | tf_op jit(solution)/shard_map/ppermute | solution.py:14
  177.8 32.0 %collective-permute-done.8 = bf16[1024,832]{0,1:T(8,128)(2,1)S(1)} collective-permute-done((bf16[1024,832]{0,1:T(8,128)(2,1)S(1)}, bf16[1024,832]{0,1:T(8,128)(2,1)S(1)}, u32[]{:S(2)}, u32[]{:S(2)}) %collective-permute-start.8) | collective-permute-done | bytes 1703968 | tf_op jit(solution)/shard_map/ppermute | solution.py:14
  210.1 2.4 exponential_convert_fusion.1
  212.5 0.8 convolution_convert_fusion.1
  213.3 4.0 %collective-permute-start.9 = (bf16[1024,64]{0,1:T(8,128)(2,1)S(1)}, bf16[1024,64]{0,1:T(8,128)(2,1)S(1)}, u32[]{:S(2)}, u32[]{:S(2)}) collective-permute-start(bf16[1024,64]{0,1:T(8,128)(2,1)S(1)} %convolution_convert_fusion.1), channel_id=1, source_target_pairs={{0,254},{1,255},{2,0},{3,1},{4,2},{5,3},{6,4},{7,5},{8,6},{9,7},{1... | collective-permute-start | bytes 393224 | tf_op jit(solution)/shard_map/ppermute | solution.py:14
  217.3 22.6 %collective-permute-done.10 = bf16[1024,832]{0,1:T(8,128)(2,1)S(1)} collective-permute-done((bf16[1024,832]{0,1:T(8,128)(2,1)S(1)}, bf16[1024,832]{0,1:T(8,128)(2,1)S(1)}, u32[]{:S(2)}, u32[]{:S(2)}) %collective-permute-start.10) | collective-permute-done | bytes 1703968 | tf_op jit(solution)/shard_map/ppermute | solution.py:14
  240.3 2.4 exponential_convert_fusion
  242.7 0.8 convolution_convert_fusion
  243.4 4.6 %collective-permute-start.11 = (bf16[1024,64]{0,1:T(8,128)(2,1)S(1)}, bf16[1024,64]{0,1:T(8,128)(2,1)S(1)}, u32[]{:S(2)}, u32[]{:S(2)}) collective-permute-start(bf16[1024,64]{0,1:T(8,128)(2,1)S(1)} %convolution_convert_fusion), channel_id=1, source_target_pairs={{0,253},{1,254},{2,255},{3,0},{4,1},{5,2},{6,3},{7,4},{8,5},{9,6},... | collective-permute-start | bytes 393224 | tf_op jit(solution)/shard_map/ppermute | solution.py:14
  248.6 0.5 fusion.20
  249.1 2.3 collective-permute-done.11
  251.4 1.3 broadcast_multiply_fusion
  (21 shorter events, 3.7 us)
Async XLA Ops:
  2.6 63.2 %collective-permute-start.4 = (bf16[1024,768]{0,1:T(8,128)(2,1)S(1)}, bf16[1024,768]{0,1:T(8,128)(2,1)S(1)}, u32[]{:S(2)}, u32[]{:S(2)}) collective-permute-start(bf16[1024,768]{0,1:T(8,128)(2,1)S(1)} %get-tuple-element.19), channel_id=1, source_target_pairs={{0,3},{1,4},{2,5},{3,6},{4,7},{5,8},{6,9},{7,10},{8,11},{9,12},{10... | collective-permute-start | bytes 4718600 | tf_op jit(solution)/shard_map/ppermute | solution.py:14
  7.1 91.7 %collective-permute-start.2 = (bf16[1024,768]{0,1:T(8,128)(2,1)S(1)}, bf16[1024,768]{0,1:T(8,128)(2,1)S(1)}, u32[]{:S(2)}, u32[]{:S(2)}) collective-permute-start(bf16[1024,768]{0,1:T(8,128)(2,1)S(1)} %get-tuple-element.19), channel_id=1, source_target_pairs={{0,2},{1,3},{2,4},{3,5},{4,6},{5,7},{6,8},{7,9},{8,10},{9,11},{10,... | collective-permute-start | bytes 4718600 | tf_op jit(solution)/shard_map/ppermute | solution.py:14
  8.7 99.0 %collective-permute-start = (bf16[1024,768]{0,1:T(8,128)(2,1)S(1)}, bf16[1024,768]{0,1:T(8,128)(2,1)S(1)}, u32[]{:S(2)}, u32[]{:S(2)}) collective-permute-start(bf16[1024,768]{0,1:T(8,128)(2,1)S(1)} %get-tuple-element.19), channel_id=1, source_target_pairs={{0,1},{1,2},{2,3},{3,4},{4,5},{5,6},{6,7},{7,8},{8,9},{9,10},{10,1... | collective-permute-start | bytes 4718600 | tf_op jit(solution)/shard_map/ppermute | solution.py:14
  108.1 20.6 %copy-start = (bf16[1024,64]{0,1:T(8,128)(2,1)S(1)}, bf16[1024,64]{0,1:T(8,128)(2,1)}, u32[]{:S(2)}) copy-start(bf16[1024,64]{0,1:T(8,128)(2,1)} %param.3) | copy-start | bytes 393220
  115.0 12.0 %collective-permute-start.1 = (f32[1024]{0:T(1024)S(1)}, f32[1024]{0:T(1024)S(1)}, u32[]{:S(2)}, u32[]{:S(2)}) collective-permute-start(f32[1024]{0:T(1024)S(1)} %get-tuple-element.6), channel_id=1, source_target_pairs={{0,255},{1,0},{2,1},{3,2},{4,3},{5,4},{6,5},{7,6},{8,7},{9,8},{10,... | collective-permute-start | bytes 12296 | tf_op jit(solution)/shard_map/ppermute | solution.py:14
  124.0 3.0 %collective-permute-start.3 = (f32[1024]{0:T(1024)S(1)}, f32[1024]{0:T(1024)S(1)}, u32[]{:S(2)}, u32[]{:S(2)}) collective-permute-start(f32[1024]{0:T(1024)S(1)} %get-tuple-element.11), channel_id=1, source_target_pairs={{0,254},{1,255},{2,0},{3,1},{4,2},{5,3},{6,4},{7,5},{8,6},{9,7},{1... | collective-permute-start | bytes 12296 | tf_op jit(solution)/shard_map/ppermute | solution.py:14
  124.8 3.9 %collective-permute-start.5 = (f32[1024]{0:T(1024)S(1)}, f32[1024]{0:T(1024)S(1)}, u32[]{:S(2)}, u32[]{:S(2)}) collective-permute-start(f32[1024]{0:T(1024)S(1)} %get-tuple-element.13), channel_id=1, source_target_pairs={{0,253},{1,254},{2,255},{3,0},{4,1},{5,2},{6,3},{7,4},{8,5},{9,6},... | collective-permute-start | bytes 12296 | tf_op jit(solution)/shard_map/ppermute | solution.py:14
  128.9 37.1 %collective-permute-start.6 = (bf16[1024,832]{0,1:T(8,128)(2,1)S(1)}, bf16[1024,832]{0,1:T(8,128)(2,1)S(1)}, u32[]{:S(2)}, u32[]{:S(2)}) collective-permute-start(bf16[1024,832]{0,1:T(8,128)(2,1)S(1)} %pad_maximum_fusion), channel_id=1, source_target_pairs={{0,1},{1,2},{2,3},{3,4},{4,5},{5,6},{6,7},{7,8},{8,9},{9,10},{10,1... | collective-permute-start | bytes 5111816 | tf_op jit(solution)/shard_map/ppermute | solution.py:14
  129.8 79.9 %collective-permute-start.8 = (bf16[1024,832]{0,1:T(8,128)(2,1)S(1)}, bf16[1024,832]{0,1:T(8,128)(2,1)S(1)}, u32[]{:S(2)}, u32[]{:S(2)}) collective-permute-start(bf16[1024,832]{0,1:T(8,128)(2,1)S(1)} %pad_maximum_fusion), channel_id=1, source_target_pairs={{0,2},{1,3},{2,4},{3,5},{4,6},{5,7},{6,8},{7,9},{8,10},{9,11},{10,... | collective-permute-start | bytes 5111816 | tf_op jit(solution)/shard_map/ppermute | solution.py:14
  129.8 110.0 %collective-permute-start.10 = (bf16[1024,832]{0,1:T(8,128)(2,1)S(1)}, bf16[1024,832]{0,1:T(8,128)(2,1)S(1)}, u32[]{:S(2)}, u32[]{:S(2)}) collective-permute-start(bf16[1024,832]{0,1:T(8,128)(2,1)S(1)} %pad_maximum_fusion), channel_id=1, source_target_pairs={{0,3},{1,4},{2,5},{3,6},{4,7},{5,8},{6,9},{7,10},{8,11},{9,12},{10... | collective-permute-start | bytes 5111816 | tf_op jit(solution)/shard_map/ppermute | solution.py:14
  169.6 79.4 %collective-permute-start.7 = (bf16[1024,64]{0,1:T(8,128)(2,1)S(1)}, bf16[1024,64]{0,1:T(8,128)(2,1)S(1)}, u32[]{:S(2)}, u32[]{:S(2)}) collective-permute-start(bf16[1024,64]{0,1:T(8,128)(2,1)S(1)} %convolution_convert_fusion.2), channel_id=1, source_target_pairs={{0,255},{1,0},{2,1},{3,2},{4,3},{5,4},{6,5},{7,6},{8,7},{9,8},{10,... | collective-permute-start | bytes 393224 | tf_op jit(solution)/shard_map/ppermute | solution.py:14
  213.3 35.8 %collective-permute-start.9 = (bf16[1024,64]{0,1:T(8,128)(2,1)S(1)}, bf16[1024,64]{0,1:T(8,128)(2,1)S(1)}, u32[]{:S(2)}, u32[]{:S(2)}) collective-permute-start(bf16[1024,64]{0,1:T(8,128)(2,1)S(1)} %convolution_convert_fusion.1), channel_id=1, source_target_pairs={{0,254},{1,255},{2,0},{3,1},{4,2},{5,3},{6,4},{7,5},{8,6},{9,7},{1... | collective-permute-start | bytes 393224 | tf_op jit(solution)/shard_map/ppermute | solution.py:14
  243.4 7.9 %collective-permute-start.11 = (bf16[1024,64]{0,1:T(8,128)(2,1)S(1)}, bf16[1024,64]{0,1:T(8,128)(2,1)S(1)}, u32[]{:S(2)}, u32[]{:S(2)}) collective-permute-start(bf16[1024,64]{0,1:T(8,128)(2,1)S(1)} %convolution_convert_fusion), channel_id=1, source_target_pairs={{0,253},{1,254},{2,255},{3,0},{4,1},{5,2},{6,3},{7,4},{8,5},{9,6},... | collective-permute-start | bytes 393224 | tf_op jit(solution)/shard_map/ppermute | solution.py:14
where the time goes:
time: 254 us; the launch traced here: 253 us
  waiting for transfers between devices  186 us (73%)
  starting transfers between devices  36.4 us (14%)
  matrix products  25.4 us (10%)
  other arithmetic  3.22 us (1%)
    ppermute x12, waiting for transfers between devices, shifted(): return lax.ppermute(value, axis, pairs)  186 us
    ppermute x12, starting transfers between devices, shifted(): return lax.ppermute(value, axis, pairs)  36.4 us
    dot_general x7, matrix products, affinity(): lax.dot_general(rows_unit, cols_unit, (((1,), (1,)), ((), ())), preferred...  19.7 us
  transfers between devices with their start and end apart: 12, of which 8 were waited for; matrix products, arithmetic and copies ran while one was open for 8% of the time, Pallas kernels for 0%

commit v1 on v0

v1 whole, which is shorter than its diff:
```python
import functools
import math

import jax
import jax.numpy as jnp
from jax import lax
from jax.experimental import pallas as pl
from jax.experimental.pallas import tpu as pltpu
from jax.sharding import PartitionSpec as P

ROUNDS = 3
MESH = pl.DeviceIdType.MESH
OWN, SIB, F1, F2, G = range(5)
CR = 256
RELAY = False
F32, BF16 = jnp.float32, jnp.bfloat16


def upward(chip):
    if not RELAY:
        return chip >= 0
    return chip // 32 < 2


class Place:
    def __init__(self, dev, count):
        wrap = lambda i: lax.rem(i + 2 * count, count)
        self.dev, self.count = dev, count
        self.core = lax.rem(dev, 2)
        chip = dev // 2
        s = 2 * self.core - 1
        self.ahead = wrap(dev + 2 * s)
        self.behind = wrap(dev - 2 * s)
        self.far = wrap(dev - 3 * s)
        self.sib = dev - s
        self.side = wrap(dev + s)
        before = lax.rem(chip + count // 2 - 1, count // 2)
        first = self.core == 0
        self.two = jnp.where(first, jnp.logical_not(upward(chip)), upward(before))
        other = jnp.where(first, upward(before), jnp.logical_not(upward(chip)))
        self.cross = jnp.where(self.two == other, self.core == 1, self.two)
        self.one = jnp.logical_not(self.two)
        self.pair = jnp.logical_not(self.cross)
        self.uses_sib = jnp.logical_or(self.one, self.pair)
        x = chip // 32
        edge = jnp.logical_and(self.core == 1, lax.rem(chip, 32) == 0)
        flipped = jnp.where(edge, x + 1 - 2 * lax.rem(x, 2), 3 - x)
        self.relay = dev + (flipped - x) * 64
        self.s = s
        self.wrap = wrap


def kernel(count, x_hbm, e_hbm, o_ref, raw, eig, blk, rel, kst, bl, dacc, dmsg, drecv, sbuf, ymsg, yrecv, yacc,
           load_sem, sib_s, sib_r, f1_s, f1_r, f2_s, f2_r, g_s, g_r, rel_s, rel_r, d_s, d_r, v_s, v_r, y_s, y_r):
    tiles, width = raw.shape
    chunks = tiles // CR
    half = chunks // 2 if RELAY else chunks
    a = math.sqrt(2.0 * width) / width * math.log2(math.e)
    me = Place(lax.axis_index("dev"), count)
    sib = Place(me.sib, count)
    side = Place(me.side, count)

    loads = [pltpu.make_async_copy(x_hbm.at[pl.ds(c * CR, CR)], raw.at[pl.ds(c * CR, CR)], load_sem.at[c]) for c in range(chunks)]
    loads.append(pltpu.make_async_copy(e_hbm, eig, load_sem.at[chunks]))
    for load in loads:
        load.start()

    partners = [me.sib, me.ahead, me.behind, me.far, me.side]
    if RELAY:
        relayed = Place(me.relay, count)
        onward = me.wrap(me.relay - 3 * me.s)
        source = Place(me.far, count).relay
        partners += [me.relay, onward, source]
    barrier = pltpu.get_barrier_semaphore()
    for partner in partners:
        pl.semaphore_signal(barrier, inc=1, device_id=(partner,), device_id_type=MESH)

    def rows(c):
        return pl.ds(c * CR if isinstance(c, int) else pl.multiple_of(c * CR, CR), CR)

    def remote(src, dst, send, recv, to):
        return pltpu.make_async_remote_copy(src_ref=src, dst_ref=dst, send_sem=send, recv_sem=recv, device_id=(to,), device_id_type=MESH)

    def to_sib(c):
        return remote(blk.at[OWN, rows(c)], blk.at[SIB, rows(c)], sib_s.at[c], sib_r.at[c], me.sib)

    def to_ahead(c):
        return remote(blk.at[OWN, rows(c)], blk.at[F1, rows(c)], f1_s.at[c], f1_r.at[c], me.ahead)

    def to_far(c):
        return remote(blk.at[OWN, rows(c)], blk.at[F2, rows(c)], f2_s.at[c], f2_r.at[c], me.far)

    def to_relay(c):
        return remote(blk.at[OWN, rows(c)], rel.at[rows(c - half)], rel_s.at[c - half], rel_r.at[c - half], me.relay)

    def to_onward(c):
        return remote(rel.at[rows(c - half)], blk.at[F2, rows(c)], f2_s.at[c], f2_r.at[c], onward)

    def to_g(c):
        return remote(blk.at[F1, rows(c)], blk.at[G, rows(c)], g_s.at[c], g_r.at[c], me.sib)

    eye = lax.broadcasted_iota(jnp.int32, (128, 128), 0) == lax.broadcasted_iota(jnp.int32, (128, 128), 1)

    def laid(column):
        parts = []
        for start in range(0, column.shape[0], 128):
            wide = jnp.broadcast_to(column[start:start + 128], (128, 128))
            parts.append(jnp.sum(jnp.where(eye, wide, 0.0), axis=0, keepdims=True))
        return jnp.concatenate(parts, axis=1)

    def offsets(unit):
        values = unit.astype(F32)
        return (0.5 * a) * jnp.sum(values * values, axis=-1, keepdims=True)

    def normalize(c):
        values = raw[rows(c), :].astype(F32)
        mean = jnp.mean(values * values, axis=-1, keepdims=True)
        unit = (values * lax.rsqrt(mean + 1e-06)).astype(BF16)
        blk[OWN, rows(c), :] = unit
        bl[OWN, :, rows(c)] = laid(offsets(unit))

    def lay_offsets(slot):
        @pl.loop(0, chunks)
        def _(c):
            bl[slot, :, rows(c)] = laid(offsets(blk[slot, rows(c), :]))

    def tile(row_slot, c, col_slot, store, diagonal=False):
        unit = blk[row_slot, rows(c), :]
        inner = lax.dot_general(unit, blk[col_slot], (((1,), (1,)), ((), ())), preferred_element_type=F32)
        value = jnp.exp2(a * inner - offsets(unit) - bl[col_slot])
        if diagonal:
            at = lax.broadcasted_iota(jnp.int32, value.shape, 0) + c * CR
            value = jnp.where(at == lax.broadcasted_iota(jnp.int32, value.shape, 1), 0.0, value)
        kst[store, rows(c), :] = value.astype(BF16)
        dacc[col_slot] += jnp.sum(value, axis=0, keepdims=True)
        if not diagonal:
            dacc[row_slot, :, rows(c)] += laid(jnp.sum(value, axis=1, keepdims=True))

    dacc[...] = jnp.zeros_like(dacc)
    for c in range(chunks):
        loads[c].wait()
        normalize(c)
        if c == 0:
            pl.semaphore_wait(barrier, len(partners))
        to_ahead(c).start()
        if RELAY and c >= half:
            @pl.when(me.one)
            def _():
                to_relay(c).start()
        to_sib(c).start()

    loads[chunks].wait()
    for c in range(tiles // 128):
        part = eig[c * 128:(c + 1) * 128, :].astype(F32)
        yacc[0, :, c * 128:(c + 1) * 128] = part.T

    @pl.loop(0, chunks)
    def _(c):
        tile(OWN, c, OWN, 0, diagonal=True)

    for c in range(chunks):
        to_sib(c).wait_recv()
    lay_offsets(SIB)

    @pl.when(me.pair)
    def _():
        @pl.loop(0, chunks)
        def _(c):
            tile(OWN, c, SIB, 3)

    @pl.loop(0, chunks)
    def _(c):
        to_ahead(c).wait_recv()

        @pl.when(sib.cross)
        def _():
            to_g(c).start()

        @pl.when(c == chunks - 2)
        def _():
            @pl.when(me.one)
            def _():
                @pl.loop(0, half)
                def _(i):
                    to_far(i).start()

            if RELAY:
                @pl.when(relayed.one)
                def _():
                    @pl.loop(half, chunks)
                    def _(i):
                        to_relay(i).wait_recv()
                        to_onward(i).start()

        tile(F1, c, OWN, 1)

        @pl.when(me.one)
        def _():
            tile(F1, c, SIB, 2)

    @pl.when(me.cross)
    def _():
        for c in range(chunks):
            to_g(c).wait_recv()
        lay_offsets(G)

        @pl.loop(0, chunks)
        def _(c):
            tile(F1, c, G, 3)

    @pl.when(me.two)
    def _():
        @pl.loop(0, chunks)
        def _(c):
            to_far(c).wait_recv()
            tile(F2, c, OWN, 2)

    def exchange(src, dst, send, recv, pick):
        holders = (
            (F1, me.behind, None, me.ahead, None),
            (G, me.side, me.cross, me.side, side.cross),
            (F2, me.far, me.two, me.far, me.one),
            (SIB, me.sib, me.uses_sib, me.sib, sib.uses_sib),
        )
        out = {}
        for slot, owner, held, holder, lent in holders:
            if pick == 0:
                out[slot] = (remote(src.at[slot], dst.at[slot], send.at[slot], recv.at[slot], owner), held, lent)
            else:
                out[slot] = (remote(src.at[OWN], dst.at[slot], send.at[slot], recv.at[slot], holder), lent, held)
        return out

    def given(condition, action):
        if condition is None:
            action()
        else:
            pl.when(condition)(action)

    degrees = exchange(dmsg, drecv, d_s, d_r, 0)
    dmsg[...] = dacc[...]
    for slot in (F1, F2, G, SIB):
        copy, sends, _ = degrees[slot]
        given(sends, copy.start)
    for slot in (SIB, G, F2, F1):
        copy, _, receives = degrees[slot]

        def add(copy=copy, slot=slot):
            copy.wait_recv()
            dacc[OWN] += drecv[slot]

        given(receives, add)
    inverse = lax.rsqrt(dacc[OWN])
    sbuf[OWN] = (yacc[0] * inverse).astype(BF16)

    scaled = exchange(sbuf, sbuf, v_s, v_r, 1)
    for slot in (G, F1, F2, SIB):
        copy, sends, _ = scaled[slot]
        given(sends, copy.start)

    def by_columns(slot, store):
        return jnp.dot(sbuf[slot], kst[store], preferred_element_type=F32)

    def by_rows(slot, store):
        return lax.dot_general(sbuf[slot], kst[store], (((1,), (1,)), ((), ())), preferred_element_type=F32)

    returned = exchange(ymsg, yrecv, y_s, y_r, 0)

    def give(slot, value):
        ymsg[slot] = value.astype(BF16)
        returned[slot][0].start()

    @pl.when(me.two)
    def _():
        give(F2, by_rows(OWN, 2))

    yacc[F1] = by_rows(OWN, 1)
    yacc[OWN] = by_columns(OWN, 0)

    @pl.when(me.pair)
    def _():
        yacc[SIB] = by_columns(OWN, 3)

    @pl.when(me.uses_sib)
    def _():
        scaled[SIB][0].wait_recv()

        @pl.when(me.one)
        def _():
            yacc[F1] += by_rows(SIB, 2)

        @pl.when(me.pair)
        def _():
            yacc[OWN] += by_rows(SIB, 3)

    @pl.when(me.cross)
    def _():
        scaled[G][0].wait_recv()
        yacc[F1] += by_rows(G, 3)

    give(F1, yacc[F1])
    scaled[F1][0].wait_recv()

    @pl.when(me.cross)
    def _():
        give(G, by_columns(F1, 3))

    @pl.when(me.uses_sib)
    def _():
        @pl.when(jnp.logical_and(me.one, me.pair))
        def _():
            yacc[SIB] += by_columns(F1, 2)

        @pl.when(jnp.logical_and(me.one, me.cross))
        def _():
            yacc[SIB] = by_columns(F1, 2)

        give(SIB, yacc[SIB])

    yacc[OWN] += by_columns(F1, 1)

    @pl.when(me.two)
    def _():
        scaled[F2][0].wait_recv()
        yacc[OWN] += by_columns(F2, 2)

    for slot in (SIB, F2, G, F1):
        copy, _, receives = returned[slot]

        def gather(copy=copy, slot=slot):
            copy.wait_recv()
            yacc[OWN] += yrecv[slot].astype(F32)

        given(receives, gather)
    factor = 0.25 * math.sqrt((2 * ROUNDS + 1) * tiles)
    o_ref[...] = (factor * inverse) * yacc[OWN]

    for c in range(chunks):
        to_ahead(c).wait_send()
        to_sib(c).wait_send()

    @pl.when(sib.cross)
    def _():
        for c in range(chunks):
            to_g(c).wait_send()

    @pl.when(me.one)
    def _():
        for c in range(half):
            to_far(c).wait_send()
        for c in range(half, chunks):
            to_relay(c).wait_send()

    if RELAY:
        @pl.when(relayed.one)
        def _():
            for c in range(half, chunks):
                to_onward(c).wait_send()

    for group in (degrees, scaled, returned):
        for copy, sends, _ in group.values():
            given(sends, copy.wait_send)


def shards(count, features, eigvecs):
    tiles, width = features.shape
    rank = eigvecs.shape[1]
    chunks = tiles // CR
    dma = lambda n: pltpu.SemaphoreType.DMA((n,))
    out = pl.pallas_call(
        functools.partial(kernel, count),
        out_shape=jax.ShapeDtypeStruct((rank, tiles), F32),
        in_specs=[pl.BlockSpec(memory_space=pl.ANY)] * 2,
        out_specs=pl.BlockSpec(memory_space=pltpu.VMEM),
        scratch_shapes=[
            pltpu.VMEM((tiles, width), BF16),
            pltpu.VMEM((tiles, rank), BF16),
            pltpu.VMEM((5, tiles, width), BF16),
            pltpu.VMEM((tiles // 2, width), BF16),
            pltpu.VMEM((4, tiles, tiles), BF16),
            pltpu.VMEM((5, 1, tiles), F32),
            pltpu.VMEM((5, 1, tiles), F32),
            pltpu.VMEM((5, 1, tiles), F32),
            pltpu.VMEM((5, 1, tiles), F32),
            pltpu.VMEM((5, rank, tiles), BF16),
            pltpu.VMEM((5, rank, tiles), BF16),
            pltpu.VMEM((5, rank, tiles), BF16),
            pltpu.VMEM((5, rank, tiles), F32),
            dma(chunks + 1),
        ] + [dma(chunks)] * 10 + [dma(5)] * 6,
        compiler_params=pltpu.CompilerParams(
            collective_id=0, has_side_effects=True, vmem_limit_bytes=56 * 2**20
        ),
        name="cluster",
    )(features, eigvecs)
    return out.T


def solution(mesh):
    return jax.shard_map(
        functools.partial(shards, mesh.shape["dev"]),
        mesh=mesh,
        in_specs=(P("dev", None), P("dev", None)),
        out_specs=P("dev", None),
        check_vma=False,
    )
```

time: 254 us -> 70.3 us (0.28)
  waiting for transfers between devices: 186 us -> 0 us
  Pallas kernels: 0 us -> 66.7 us
  starting transfers between devices: 36.4 us -> 0 us
  matrix products: 25.4 us -> 0 us
  other arithmetic: 3.22 us -> 0 us
    ppermute x12 -> x0, waiting for transfers between devices: 186 us -> none  [shifted(): return lax.ppermute(value, axis, pairs)]
    pallas_call x0 -> x1, Pallas kernels: none -> 66.7 us  [shards(): pl.pallas_call(functools.partial(kernel, count), out_shape=jax.ShapeDtype...]
    ppermute x12 -> x0, starting transfers between devices: 36.4 us -> none  [shifted(): return lax.ppermute(value, axis, pairs)]
    dot_general x14 -> x0, matrix products: 25.4 us -> none  [the longest x7 19.7 us: affinity(): lax.dot_general(rows_unit, cols_unit, (((1,), (1,)), ((), ())), preferred...]
    reduce_sum x8 -> x0, other arithmetic: 3.04 us -> none  [the longest x7 2.68 us: squares(): return jnp.sum(values * values, axis=-1)]
  transfers between devices with their start and end apart: 12 -> 0, of which waited for: 8 -> 0; matrix products, arithmetic and copies ran while one was open for 8% -> 0% of each run, Pallas kernels for 0% -> 0%
where the time goes in v1:
time: 70.3 us; the launch traced here: 70.2 us
  Pallas kernels  66.7 us (95%)
  local copies, waits for them, and re-layouts  3.42 us (5%)
    pallas_call x1, Pallas kernels, shards(): pl.pallas_call(functools.partial(kernel, count), out_shape=jax.ShapeDtype...  66.7 us
    unnamed x2, local copies, waits for them, and re-layouts  3.42 us

profile of v1, /device:TPU:1, one launch (start us, length us, event | category | flops | bytes accessed | tf_op | source)
XLA Modules:
  0.0 70.2 jit_solution(1197621662071146241)
XLA Ops:
  0.0 1.7 %copy.3.e_hbm = bf16[1024,64]{1,0:T(8,128)(2,1)} copy(bf16[1024,64]{0,1:T(8,128)(2,1)} %param.3) | data formatting | bytes 262144 | tf_op args[1]
  1.7 66.7 %cluster.1 = f32[64,1024]{1,0:T(8,128)} custom-call(bf16[1024,768]{1,0:T(8,128)(2,1)} %x_hbm.1, bf16[1024,64]{1,0:T(8,128)(2,1)} %copy.3.e_hbm), custom_call_target="tpu_custom_call" | custom-call | tf_op jit(solution)/shard_map/cluster/pallas_call | solution.py:369
  68.5 1.7 %copy.5 = f32[1024,64]{0,1:T(8,128)} copy(f32[1024,64]{0,1:T(8,128)} %bitcast.1) | data formatting | bytes 524288

commit v2 on v1

--- a/solution.py
+++ b/solution.py
@@ -12,14 +12,14 @@
 MESH = pl.DeviceIdType.MESH
 OWN, SIB, F1, F2, G = range(5)
 CR = 256
-RELAY = False
+RELAY = True
 F32, BF16 = jnp.float32, jnp.bfloat16
 
 
-def upward(chip):
+def upward(chip, count):
     if not RELAY:
         return chip >= 0
-    return chip // 32 < 2
+    return chip < count // 4
 
 
 class Place:
@@ -36,16 +36,17 @@
         self.side = wrap(dev + s)
         before = lax.rem(chip + count // 2 - 1, count // 2)
         first = self.core == 0
-        self.two = jnp.where(first, jnp.logical_not(upward(chip)), upward(before))
-        other = jnp.where(first, upward(before), jnp.logical_not(upward(chip)))
+        self.two = jnp.where(first, jnp.logical_not(upward(chip, count)), upward(before, count))
+        other = jnp.where(first, upward(before, count), jnp.logical_not(upward(chip, count)))
         self.cross = jnp.where(self.two == other, self.core == 1, self.two)
         self.one = jnp.logical_not(self.two)
         self.pair = jnp.logical_not(self.cross)
         self.uses_sib = jnp.logical_or(self.one, self.pair)
-        x = chip // 32
-        edge = jnp.logical_and(self.core == 1, lax.rem(chip, 32) == 0)
+        plane = count // 8
+        x = chip // plane
+        edge = jnp.logical_and(self.core == 1, lax.rem(chip, plane) == 0)
         flipped = jnp.where(edge, x + 1 - 2 * lax.rem(x, 2), 3 - x)
-        self.relay = dev + (flipped - x) * 64
+        self.relay = dev + (flipped - x) * 2 * plane
         self.s = s
         self.wrap = wrap
 
@@ -150,9 +151,7 @@
         to_sib(c).start()
 
     loads[chunks].wait()
-    for c in range(tiles // 128):
-        part = eig[c * 128:(c + 1) * 128, :].astype(F32)
-        yacc[0, :, c * 128:(c + 1) * 128] = part.T
+    yacc[0] = eig[...].astype(F32)
 
     @pl.loop(0, chunks)
     def _(c):
@@ -373,7 +372,7 @@
         out_specs=pl.BlockSpec(memory_space=pltpu.VMEM),
         scratch_shapes=[
             pltpu.VMEM((tiles, width), BF16),
-            pltpu.VMEM((tiles, rank), BF16),
+            pltpu.VMEM((rank, tiles), BF16),
             pltpu.VMEM((5, tiles, width), BF16),
             pltpu.VMEM((tiles // 2, width), BF16),
             pltpu.VMEM((4, tiles, tiles), BF16),
@@ -391,7 +390,7 @@
             collective_id=0, has_side_effects=True, vmem_limit_bytes=56 * 2**20
         ),
         name="cluster",
-    )(features, eigvecs)
+    )(features, eigvecs.T)
     return out.T
 
 

time: 70.3 us -> 79.1 us (1.13)
  the two profiles are of different devices: /device:TPU:1 before, /device:TPU:26 now
where the time goes in v2:
time: 79.1 us; the launch traced here: 79 us
  Pallas kernels  77.3 us (98%)
  local copies, waits for them, and re-layouts  1.67 us (2%)
    pallas_call x1, Pallas kernels, shards(): pl.pallas_call(functools.partial(kernel, count), out_shape=jax.ShapeDtype...  77.3 us
    unnamed x1, local copies, waits for them, and re-layouts  1.67 us

profile of v2, /device:TPU:26, one launch (start us, length us, event | category | flops | bytes accessed | tf_op | source)
XLA Modules:
  0.0 79.0 jit_solution(6434963265233862377)
XLA Ops:
  0.0 77.3 %cluster.1 = f32[64,1024]{1,0:T(8,128)} custom-call(bf16[1024,768]{1,0:T(8,128)(2,1)} %x_hbm.1, bf16[64,1024]{1,0:T(8,128)(2,1)} %bitcast.3), custom_call_target="tpu_custom_call" | custom-call | tf_op jit(solution)/shard_map/cluster/pallas_call | solution.py:368
  77.3 1.7 %copy.4 = f32[1024,64]{0,1:T(8,128)} copy(f32[1024,64]{0,1:T(8,128)} %bitcast.2) | data formatting | bytes 524288

commit v3 on v2

--- a/solution.py
+++ b/solution.py
@@ -12,50 +12,54 @@
 MESH = pl.DeviceIdType.MESH
 OWN, SIB, F1, F2, G = range(5)
 CR = 256
-RELAY = True
+DIMS = (4, 4, 8)
 F32, BF16 = jnp.float32, jnp.bfloat16
 
 
-def upward(chip, count):
-    if not RELAY:
-        return chip >= 0
-    return chip < count // 4
+def upward(chip):
+    x, y, z = chip // (DIMS[1] * DIMS[2]), lax.rem(chip // DIMS[2], DIMS[1]), lax.rem(chip, DIMS[2])
+    return jnp.where(z < DIMS[2] - 1, x < DIMS[0] // 2, lax.rem(y, 2) == 0)
 
 
 class Place:
     def __init__(self, dev, count):
         wrap = lambda i: lax.rem(i + 2 * count, count)
-        self.dev, self.count = dev, count
-        self.core = lax.rem(dev, 2)
+        self.dev, self.count, self.wrap = dev, count, wrap
+        core = lax.rem(dev, 2)
         chip = dev // 2
-        s = 2 * self.core - 1
+        s = 2 * core - 1
+        self.s = s
         self.ahead = wrap(dev + 2 * s)
         self.behind = wrap(dev - 2 * s)
         self.far = wrap(dev - 3 * s)
         self.sib = dev - s
         self.side = wrap(dev + s)
         before = lax.rem(chip + count // 2 - 1, count // 2)
-        first = self.core == 0
-        self.two = jnp.where(first, jnp.logical_not(upward(chip, count)), upward(before, count))
-        other = jnp.where(first, upward(before, count), jnp.logical_not(upward(chip, count)))
-        self.cross = jnp.where(self.two == other, self.core == 1, self.two)
+        first = core == 0
+        self.two = jnp.where(first, jnp.logical_not(upward(chip)), upward(before))
+        other = jnp.where(first, upward(before), jnp.logical_not(upward(chip)))
+        self.cross = jnp.where(self.two == other, core == 1, self.two)
         self.one = jnp.logical_not(self.two)
         self.pair = jnp.logical_not(self.cross)
         self.uses_sib = jnp.logical_or(self.one, self.pair)
-        plane = count // 8
-        x = chip // plane
-        edge = jnp.logical_and(self.core == 1, lax.rem(chip, plane) == 0)
-        flipped = jnp.where(edge, x + 1 - 2 * lax.rem(x, 2), 3 - x)
-        self.relay = dev + (flipped - x) * 2 * plane
-        self.s = s
-        self.wrap = wrap
+        x, y, z = chip // (DIMS[1] * DIMS[2]), lax.rem(chip // DIMS[2], DIMS[1]), lax.rem(chip, DIMS[2])
+        turn = jnp.where(first, z == DIMS[2] - 1, z == 0)
+        across = dev + (DIMS[0] - 1 - 2 * x) * (2 * DIMS[1] * DIMS[2])
+        self.relay = jnp.where(turn, wrap(dev - s * 2 * DIMS[2]), across)
+        self.source = jnp.where(turn, wrap(dev + s * 2 * DIMS[2]), across)
+        low = z - core
+        kept = jnp.logical_and(
+            jnp.logical_or(y == 0, y == DIMS[1] - 1),
+            jnp.logical_or(low == 0, low == DIMS[2] - 2),
+        )
+        self.split = jnp.logical_and(self.one, jnp.logical_or(turn, jnp.logical_not(kept)))
 
 
 def kernel(count, x_hbm, e_hbm, o_ref, raw, eig, blk, rel, kst, bl, dacc, dmsg, drecv, sbuf, ymsg, yrecv, yacc,
            load_sem, sib_s, sib_r, f1_s, f1_r, f2_s, f2_r, g_s, g_r, rel_s, rel_r, d_s, d_r, v_s, v_r, y_s, y_r):
     tiles, width = raw.shape
     chunks = tiles // CR
-    half = chunks // 2 if RELAY else chunks
+    half = chunks // 2
     a = math.sqrt(2.0 * width) / width * math.log2(math.e)
     me = Place(lax.axis_index("dev"), count)
     sib = Place(me.sib, count)
@@ -67,11 +71,9 @@
         load.start()
 
     partners = [me.sib, me.ahead, me.behind, me.far, me.side]
-    if RELAY:
-        relayed = Place(me.relay, count)
-        onward = me.wrap(me.relay - 3 * me.s)
-        source = Place(me.far, count).relay
-        partners += [me.relay, onward, source]
+    source = Place(me.source, count)
+    onward = source.far
+    partners += [me.relay, me.source, onward, Place(me.far, count).relay]
     barrier = pltpu.get_barrier_semaphore()
     for partner in partners:
         pl.semaphore_signal(barrier, inc=1, device_id=(partner,), device_id_type=MESH)
@@ -144,8 +146,8 @@
         if c == 0:
             pl.semaphore_wait(barrier, len(partners))
         to_ahead(c).start()
-        if RELAY and c >= half:
-            @pl.when(me.one)
+        if c >= half:
+            @pl.when(me.split)
             def _():
                 to_relay(c).start()
         to_sib(c).start()
@@ -183,13 +185,18 @@
                 def _(i):
                     to_far(i).start()
 
-            if RELAY:
-                @pl.when(relayed.one)
-                def _():
-                    @pl.loop(half, chunks)
-                    def _(i):
-                        to_relay(i).wait_recv()
-                        to_onward(i).start()
+            @pl.when(me.one & jnp.logical_not(me.split))
+            def _():
+                @pl.loop(half, chunks)
+                def _(i):
+                    to_far(i).start()
+
+            @pl.when(source.split)
+            def _():
+                @pl.loop(half, chunks)
+                def _(i):
+                    to_relay(i).wait_recv()
+                    to_onward(i).start()
 
         tile(F1, c, OWN, 1)
 
@@ -210,7 +217,8 @@
     @pl.when(me.two)
     def _():
         @pl.loop(0, chunks)
-        def _(c):
+        def _(i):
+            c = i // 2 + lax.rem(i, 2) * half
             to_far(c).wait_recv()
             tile(F2, c, OWN, 2)
 
@@ -346,14 +354,21 @@
     def _():
         for c in range(half):
             to_far(c).wait_send()
+
+    @pl.when(me.one & jnp.logical_not(me.split))
+    def _():
+        for c in range(half, chunks):
+            to_far(c).wait_send()
+
+    @pl.when(me.split)
+    def _():
         for c in range(half, chunks):
             to_relay(c).wait_send()
 
-    if RELAY:
-        @pl.when(relayed.one)
-        def _():
-            for c in range(half, chunks):
-                to_onward(c).wait_send()
+    @pl.when(source.split)
+    def _():
+        for c in range(half, chunks):
+            to_onward(c).wait_send()
 
     for group in (degrees, scaled, returned):
         for copy, sends, _ in group.values():

time: 79.1 us -> 64.6 us (0.82)
  the two profiles are of different devices: /device:TPU:26 before, /device:TPU:2 now
where the time goes in v3:
time: 64.6 us; the launch traced here: 64.5 us
  Pallas kernels  62.8 us (97%)
  local copies, waits for them, and re-layouts  1.67 us (3%)
    pallas_call x1, Pallas kernels, shards(): pl.pallas_call(functools.partial(kernel, count), out_shape=jax.ShapeDtype...  62.8 us
    unnamed x1, local copies, waits for them, and re-layouts  1.67 us

profile of v3, /device:TPU:2, one launch (start us, length us, event | category | flops | bytes accessed | tf_op | source)
XLA Modules:
  0.0 64.5 jit_solution(13420379099622906932)
XLA Ops:
  0.0 62.8 %cluster.1 = f32[64,1024]{1,0:T(8,128)} custom-call(bf16[1024,768]{1,0:T(8,128)(2,1)} %x_hbm.1, bf16[64,1024]{1,0:T(8,128)(2,1)} %bitcast.3), custom_call_target="tpu_custom_call" | custom-call | tf_op jit(solution)/shard_map/cluster/pallas_call | solution.py:383
  62.8 1.7 %copy.4 = f32[1024,64]{0,1:T(8,128)} copy(f32[1024,64]{0,1:T(8,128)} %bitcast.2) | data formatting | bytes 524288

commit v4 on v3

--- a/solution.py
+++ b/solution.py
@@ -18,7 +18,9 @@
 
 def upward(chip):
     x, y, z = chip // (DIMS[1] * DIMS[2]), lax.rem(chip // DIMS[2], DIMS[1]), lax.rem(chip, DIMS[2])
-    return jnp.where(z < DIMS[2] - 1, x < DIMS[0] // 2, lax.rem(y, 2) == 0)
+    outer = (y == 0) | (y == DIMS[1] - 1)
+    middle = (x == DIMS[0] // 2 - 1) | (x == DIMS[0] // 2)
+    return jnp.where(z < DIMS[2] - 1, (x < DIMS[0] // 2) != (outer & middle), lax.rem(y, 2) == 0)
 
 
 class Place:
@@ -47,16 +49,10 @@
         across = dev + (DIMS[0] - 1 - 2 * x) * (2 * DIMS[1] * DIMS[2])
         self.relay = jnp.where(turn, wrap(dev - s * 2 * DIMS[2]), across)
         self.source = jnp.where(turn, wrap(dev + s * 2 * DIMS[2]), across)
-        low = z - core
-        kept = jnp.logical_and(
-            jnp.logical_or(y == 0, y == DIMS[1] - 1),
-            jnp.logical_or(low == 0, low == DIMS[2] - 2),
-        )
-        self.split = jnp.logical_and(self.one, jnp.logical_or(turn, jnp.logical_not(kept)))
-
-
-def kernel(count, x_hbm, e_hbm, o_ref, raw, eig, blk, rel, kst, bl, dacc, dmsg, drecv, sbuf, ymsg, yrecv, yacc,
-           load_sem, sib_s, sib_r, f1_s, f1_r, f2_s, f2_r, g_s, g_r, rel_s, rel_r, d_s, d_r, v_s, v_r, y_s, y_r):
+
+
+def kernel(count, x_hbm, e_hbm, o_ref, raw, blk, rel, kst, bl, dacc, total, drecv, ebuf, sbuf, ymsg, yrecv, yacc,
+           load_sem, sib_s, sib_r, f1_s, f1_r, f2_s, f2_r, g_s, g_r, rel_s, rel_r, e_s, e_r, y_s, y_r, d_s, d_r):
     tiles, width = raw.shape
     chunks = tiles // CR
     half = chunks // 2
@@ -66,11 +62,11 @@
     side = Place(me.side, count)
 
     loads = [pltpu.make_async_copy(x_hbm.at[pl.ds(c * CR, CR)], raw.at[pl.ds(c * CR, CR)], load_sem.at[c]) for c in range(chunks)]
-    loads.append(pltpu.make_async_copy(e_hbm, eig, load_sem.at[chunks]))
+    loads.append(pltpu.make_async_copy(e_hbm, ebuf.at[OWN], load_sem.at[chunks]))
     for load in loads:
         load.start()
 
-    partners = [me.sib, me.ahead, me.behind, me.far, me.side]
+    partners = [me.wrap(me.dev + step) for step in (1, -1, 2, -2, 3, -3, 4, -4, 5, -5)]
     source = Place(me.source, count)
     onward = source.far
     partners += [me.relay, me.source, onward, Place(me.far, count).relay]
@@ -147,13 +143,23 @@
             pl.semaphore_wait(barrier, len(partners))
         to_ahead(c).start()
         if c >= half:
-            @pl.when(me.split)
+            @pl.when(me.one)
             def _():
                 to_relay(c).start()
         to_sib(c).start()
 
     loads[chunks].wait()
-    yacc[0] = eig[...].astype(F32)
+
+    def eig_to(slot, to):
+        return remote(ebuf.at[OWN], ebuf.at[slot], e_s.at[slot], e_r.at[slot], to)
+
+    eig_ahead, eig_far, eig_sib = eig_to(F1, me.ahead), eig_to(F2, me.far), eig_to(SIB, me.sib)
+    eig_g = remote(ebuf.at[F1], ebuf.at[G], e_s.at[G], e_r.at[G], me.sib)
+    eig_ahead.start()
+
+    @pl.when(sib.uses_sib)
+    def _():
+        eig_sib.start()
 
     @pl.loop(0, chunks)
     def _(c):
@@ -181,17 +187,13 @@
         def _():
             @pl.when(me.one)
             def _():
+                eig_far.start()
+
                 @pl.loop(0, half)
                 def _(i):
                     to_far(i).start()
 
-            @pl.when(me.one & jnp.logical_not(me.split))
-            def _():
-                @pl.loop(half, chunks)
-                def _(i):
-                    to_far(i).start()
-
-            @pl.when(source.split)
+            @pl.when(source.one)
             def _():
                 @pl.loop(half, chunks)
                 def _(i):
@@ -204,6 +206,12 @@
         def _():
             tile(F1, c, SIB, 2)
 
+    eig_ahead.wait_recv()
+
+    @pl.when(sib.cross)
+    def _():
+        eig_g.start()
+
     @pl.when(me.cross)
     def _():
         for c in range(chunks):
@@ -213,6 +221,45 @@
         @pl.loop(0, chunks)
         def _(c):
             tile(F1, c, G, 3)
+
+    owners = {OWN: me, F1: Place(me.behind, count), G: side, F2: Place(me.far, count), SIB: sib}
+    held = {OWN: None, F1: None, G: me.cross, F2: me.two, SIB: me.uses_sib}
+
+    def member(owner, kind):
+        if kind == OWN:
+            return owner.dev, None
+        if kind == F1:
+            return owner.ahead, None
+        if kind == G:
+            return owner.side, Place(owner.side, count).cross
+        if kind == F2:
+            return owner.far, owner.one
+        return owner.sib, Place(owner.sib, count).uses_sib
+
+    def given(conditions, action):
+        known = [c for c in conditions if c is not None]
+        if known:
+            pl.when(functools.reduce(jnp.logical_and, known))(action)
+        else:
+            action()
+
+    def part(slot, kind):
+        dev, exists = member(owners[slot], kind)
+        out = lambda: remote(dacc.at[slot], drecv.at[kind, slot], d_s.at[slot, kind], d_r.at[kind, slot], dev)
+        back = lambda: remote(dacc.at[kind], drecv.at[slot, kind], d_s.at[kind, slot], d_r.at[slot, kind], dev)
+        return out, back, (held[slot], exists)
+
+    kinds = (OWN, F1, G, F2, SIB)
+
+    def send_parts(slot):
+        for kind in kinds:
+            if kind != slot:
+                out, _, when = part(slot, kind)
+                given(when, lambda: out().start())
+
+    send_parts(F1)
+    send_parts(G)
+    send_parts(SIB)
 
     @pl.when(me.two)
     def _():
@@ -222,47 +269,21 @@
             to_far(c).wait_recv()
             tile(F2, c, OWN, 2)
 
-    def exchange(src, dst, send, recv, pick):
-        holders = (
-            (F1, me.behind, None, me.ahead, None),
-            (G, me.side, me.cross, me.side, side.cross),
-            (F2, me.far, me.two, me.far, me.one),
-            (SIB, me.sib, me.uses_sib, me.sib, sib.uses_sib),
-        )
-        out = {}
-        for slot, owner, held, holder, lent in holders:
-            if pick == 0:
-                out[slot] = (remote(src.at[slot], dst.at[slot], send.at[slot], recv.at[slot], owner), held, lent)
-            else:
-                out[slot] = (remote(src.at[OWN], dst.at[slot], send.at[slot], recv.at[slot], holder), lent, held)
-        return out
-
-    def given(condition, action):
-        if condition is None:
-            action()
-        else:
-            pl.when(condition)(action)
-
-    degrees = exchange(dmsg, drecv, d_s, d_r, 0)
-    dmsg[...] = dacc[...]
-    for slot in (F1, F2, G, SIB):
-        copy, sends, _ = degrees[slot]
-        given(sends, copy.start)
-    for slot in (SIB, G, F2, F1):
-        copy, _, receives = degrees[slot]
-
-        def add(copy=copy, slot=slot):
-            copy.wait_recv()
-            dacc[OWN] += drecv[slot]
-
-        given(receives, add)
-    inverse = lax.rsqrt(dacc[OWN])
-    sbuf[OWN] = (yacc[0] * inverse).astype(BF16)
-
-    scaled = exchange(sbuf, sbuf, v_s, v_r, 1)
-    for slot in (G, F1, F2, SIB):
-        copy, sends, _ = scaled[slot]
-        given(sends, copy.start)
+    send_parts(OWN)
+    send_parts(F2)
+
+    def scale(slot):
+        for kind in kinds:
+            if kind != slot:
+                _, back, when = part(slot, kind)
+
+                def add(back=back, kind=kind):
+                    back().wait_recv()
+                    total[slot] += drecv[slot, kind]
+
+                given(when, add)
+        inverse = lax.rsqrt(total[slot])
+        sbuf[slot] = (ebuf[slot].astype(F32) * inverse).astype(BF16)
 
     def by_columns(slot, store):
         return jnp.dot(sbuf[slot], kst[store], preferred_element_type=F32)
@@ -270,74 +291,81 @@
     def by_rows(slot, store):
         return lax.dot_general(sbuf[slot], kst[store], (((1,), (1,)), ((), ())), preferred_element_type=F32)
 
-    returned = exchange(ymsg, yrecv, y_s, y_r, 0)
+    def returns(slot):
+        out = remote(ymsg.at[slot], yrecv.at[slot], y_s.at[slot], y_r.at[slot], owners[slot].dev)
+        return out, held[slot], member(me, slot)[1]
 
     def give(slot, value):
         ymsg[slot] = value.astype(BF16)
-        returned[slot][0].start()
+        returns(slot)[0].start()
+
+    total[...] = dacc[...]
+    scale(OWN)
 
     @pl.when(me.two)
     def _():
         give(F2, by_rows(OWN, 2))
 
     yacc[F1] = by_rows(OWN, 1)
+
+    @pl.when(me.uses_sib)
+    def _():
+        eig_sib.wait_recv()
+        scale(SIB)
+
+        @pl.when(me.one)
+        def _():
+            yacc[F1] += by_rows(SIB, 2)
+
+    @pl.when(me.cross)
+    def _():
+        eig_g.wait_recv()
+        scale(G)
+        yacc[F1] += by_rows(G, 3)
+
+    give(F1, yacc[F1])
+    scale(F1)
+
+    @pl.when(me.cross)
+    def _():
+        give(G, by_columns(F1, 3))
+
+    @pl.when(me.uses_sib)
+    def _():
+        yacc[SIB] = jnp.zeros_like(yacc[SIB])
+
+        @pl.when(me.one)
+        def _():
+            yacc[SIB] += by_columns(F1, 2)
+
+        @pl.when(me.pair)
+        def _():
+            yacc[SIB] += by_columns(OWN, 3)
+
+        give(SIB, yacc[SIB])
+
     yacc[OWN] = by_columns(OWN, 0)
+    yacc[OWN] += by_columns(F1, 1)
+
+    @pl.when(me.two)
+    def _():
+        eig_far.wait_recv()
+        scale(F2)
+        yacc[OWN] += by_columns(F2, 2)
 
     @pl.when(me.pair)
     def _():
-        yacc[SIB] = by_columns(OWN, 3)
-
-    @pl.when(me.uses_sib)
-    def _():
-        scaled[SIB][0].wait_recv()
-
-        @pl.when(me.one)
-        def _():
-            yacc[F1] += by_rows(SIB, 2)
-
-        @pl.when(me.pair)
-        def _():
-            yacc[OWN] += by_rows(SIB, 3)
-
-    @pl.when(me.cross)
-    def _():
-        scaled[G][0].wait_recv()
-        yacc[F1] += by_rows(G, 3)
-
-    give(F1, yacc[F1])
-    scaled[F1][0].wait_recv()
-
-    @pl.when(me.cross)
-    def _():
-        give(G, by_columns(F1, 3))
-
-    @pl.when(me.uses_sib)
-    def _():
-        @pl.when(jnp.logical_and(me.one, me.pair))
-        def _():
-            yacc[SIB] += by_columns(F1, 2)
-
-        @pl.when(jnp.logical_and(me.one, me.cross))
-        def _():
-            yacc[SIB] = by_columns(F1, 2)
-
-        give(SIB, yacc[SIB])
-
-    yacc[OWN] += by_columns(F1, 1)
-
-    @pl.when(me.two)
-    def _():
-        scaled[F2][0].wait_recv()
-        yacc[OWN] += by_columns(F2, 2)
+        yacc[OWN] += by_rows(SIB, 3)
 
     for slot in (SIB, F2, G, F1):
-        copy, _, receives = returned[slot]
+        copy, _, receives = returns(slot)
 
         def gather(copy=copy, slot=slot):
             copy.wait_recv()
             yacc[OWN] += yrecv[slot].astype(F32)
 
-        given(receives, gather)
+        given((receives,), gather)
+    inverse = lax.rsqrt(total[OWN])
     factor = 0.25 * math.sqrt((2 * ROUNDS + 1) * tiles)
     o_ref[...] = (factor * inverse) * yacc[OWN]
 
@@ -355,24 +383,28 @@
         for c in range(half):
             to_far(c).wait_send()
 
-    @pl.when(me.one & jnp.logical_not(me.split))
-    def _():
-        for c in range(half, chunks):
-            to_far(c).wait_send()
-
-    @pl.when(me.split)
+    @pl.when(me.one)
     def _():
         for c in range(half, chunks):
             to_relay(c).wait_send()
 
-    @pl.when(source.split)
+    @pl.when(source.one)
     def _():
         for c in range(half, chunks):
             to_onward(c).wait_send()
 
-    for group in (degrees, scaled, returned):
-        for copy, sends, _ in group.values():
-            given(sends, copy.wait_send)
+    eig_ahead.wait_send()
+    given((sib.uses_sib,), eig_sib.wait_send)
+    given((me.one,), eig_far.wait_send)
+    given((sib.cross,), eig_g.wait_send)
+    for slot in kinds:
+        for kind in kinds:
+            if kind != slot:
+                out, _, when = part(slot, kind)
+                given(when, lambda: out().wait_send())
+        if slot != OWN:
+            copy, sends, _ = returns(slot)
+            given((sends,), copy.wait_send)
 
 
 def shards(count, features, eigvecs):
@@ -387,20 +419,20 @@
         out_specs=pl.BlockSpec(memory_space=pltpu.VMEM),
         scratch_shapes=[
             pltpu.VMEM((tiles, width), BF16),
-            pltpu.VMEM((rank, tiles), BF16),
             pltpu.VMEM((5, tiles, width), BF16),
             pltpu.VMEM((tiles // 2, width), BF16),
             pltpu.VMEM((4, tiles, tiles), BF16),
             pltpu.VMEM((5, 1, tiles), F32),
             pltpu.VMEM((5, 1, tiles), F32),
             pltpu.VMEM((5, 1, tiles), F32),
-            pltpu.VMEM((5, 1, tiles), F32),
+            pltpu.VMEM((5, 5, 1, tiles), F32),
+            pltpu.VMEM((5, rank, tiles), BF16),
             pltpu.VMEM((5, rank, tiles), BF16),
             pltpu.VMEM((5, rank, tiles), BF16),
             pltpu.VMEM((5, rank, tiles), BF16),
             pltpu.VMEM((5, rank, tiles), F32),
             dma(chunks + 1),
-        ] + [dma(chunks)] * 10 + [dma(5)] * 6,
+        ] + [dma(chunks)] * 10 + [dma(5)] * 4 + [pltpu.SemaphoreType.DMA((5, 5))] * 2,
         compiler_params=pltpu.CompilerParams(
             collective_id=0, has_side_effects=True, vmem_limit_bytes=56 * 2**20
         ),

time: 64.6 us -> 61 us (0.944)
  the two profiles are of different devices: /device:TPU:2 before, /device:TPU:1 now
where the time goes in v4:
time: 61 us; the launch traced here: 60.9 us
  Pallas kernels  59.2 us (97%)
  local copies, waits for them, and re-layouts  1.67 us (3%)
    pallas_call x1, Pallas kernels, shards(): pl.pallas_call(functools.partial(kernel, count), out_shape=jax.ShapeDtype...  59.2 us
    unnamed x1, local copies, waits for them, and re-layouts  1.67 us

profile of v4, /device:TPU:1, one launch (start us, length us, event | category | flops | bytes accessed | tf_op | source)
XLA Modules:
  0.0 60.9 jit_solution(7994295538202611736)
XLA Ops:
  0.0 59.2 %cluster.1 = f32[64,1024]{1,0:T(8,128)} custom-call(bf16[1024,768]{1,0:T(8,128)(2,1)} %x_hbm.1, bf16[64,1024]{1,0:T(8,128)(2,1)} %bitcast.3), custom_call_target="tpu_custom_call" | custom-call | tf_op jit(solution)/shard_map/cluster/pallas_call | solution.py:415
  59.2 1.7 %copy.4 = f32[1024,64]{0,1:T(8,128)} copy(f32[1024,64]{0,1:T(8,128)} %bitcast.2) | data formatting | bytes 524288

commit v5 on v4

--- a/solution.py
+++ b/solution.py
@@ -66,7 +66,7 @@
     for load in loads:
         load.start()
 
-    partners = [me.wrap(me.dev + step) for step in (1, -1, 2, -2, 3, -3, 4, -4, 5, -5)]
+    partners = [me.sib, me.side, me.ahead, me.behind, me.far]
     source = Place(me.source, count)
     onward = source.far
     partners += [me.relay, me.source, onward, Place(me.far, count).relay]
@@ -116,31 +116,31 @@
         mean = jnp.mean(values * values, axis=-1, keepdims=True)
         unit = (values * lax.rsqrt(mean + 1e-06)).astype(BF16)
         blk[OWN, rows(c), :] = unit
-        bl[OWN, :, rows(c)] = laid(offsets(unit))
+        bl[OWN, rows(c), :] = jnp.broadcast_to(offsets(unit), (CR, 128))
 
     def lay_offsets(slot):
         @pl.loop(0, chunks)
         def _(c):
-            bl[slot, :, rows(c)] = laid(offsets(blk[slot, rows(c), :]))
-
-    def tile(row_slot, c, col_slot, store, diagonal=False):
-        unit = blk[row_slot, rows(c), :]
-        inner = lax.dot_general(unit, blk[col_slot], (((1,), (1,)), ((), ())), preferred_element_type=F32)
-        value = jnp.exp2(a * inner - offsets(unit) - bl[col_slot])
+            bl[slot, rows(c), :] = jnp.broadcast_to(offsets(blk[slot, rows(c), :]), (CR, 128))
+
+    def tile(row_slot, col_slot, c, store, diagonal=False):
+        unit = blk[col_slot, rows(c), :]
+        inner = lax.dot_general(blk[row_slot], unit, (((1,), (1,)), ((), ())), preferred_element_type=F32)
+        value = jnp.exp2(a * inner - jnp.concatenate([bl[row_slot]] * (CR // 128), axis=1) - laid(offsets(unit)))
         if diagonal:
-            at = lax.broadcasted_iota(jnp.int32, value.shape, 0) + c * CR
-            value = jnp.where(at == lax.broadcasted_iota(jnp.int32, value.shape, 1), 0.0, value)
-        kst[store, rows(c), :] = value.astype(BF16)
-        dacc[col_slot] += jnp.sum(value, axis=0, keepdims=True)
+            at = lax.broadcasted_iota(jnp.int32, value.shape, 1) + c * CR
+            value = jnp.where(at == lax.broadcasted_iota(jnp.int32, value.shape, 0), 0.0, value)
+        kst[store, :, rows(c)] = value.astype(BF16)
+        dacc[col_slot, :, rows(c)] += jnp.sum(value, axis=0, keepdims=True)
         if not diagonal:
-            dacc[row_slot, :, rows(c)] += laid(jnp.sum(value, axis=1, keepdims=True))
+            dacc[row_slot] += laid(jnp.sum(value, axis=1, keepdims=True))
 
     dacc[...] = jnp.zeros_like(dacc)
     for c in range(chunks):
         loads[c].wait()
         normalize(c)
-        if c == 0:
-            pl.semaphore_wait(barrier, len(partners))
+    pl.semaphore_wait(barrier, len(partners))
+    for c in range(chunks):
         to_ahead(c).start()
         if c >= half:
             @pl.when(me.one)
@@ -155,15 +155,13 @@
 
     eig_ahead, eig_far, eig_sib = eig_to(F1, me.ahead), eig_to(F2, me.far), eig_to(SIB, me.sib)
     eig_g = remote(ebuf.at[F1], ebuf.at[G], e_s.at[G], e_r.at[G], me.sib)
-    eig_ahead.start()
-
     @pl.when(sib.uses_sib)
     def _():
         eig_sib.start()
 
     @pl.loop(0, chunks)
     def _(c):
-        tile(OWN, c, OWN, 0, diagonal=True)
+        tile(OWN, OWN, c, 0, diagonal=True)
 
     for c in range(chunks):
         to_sib(c).wait_recv()
@@ -173,7 +171,7 @@
     def _():
         @pl.loop(0, chunks)
         def _(c):
-            tile(OWN, c, SIB, 3)
+            tile(OWN, SIB, c, 3)
 
     @pl.loop(0, chunks)
     def _(c):
@@ -187,8 +185,6 @@
         def _():
             @pl.when(me.one)
             def _():
-                eig_far.start()
-
                 @pl.loop(0, half)
                 def _(i):
                     to_far(i).start()
@@ -200,17 +196,11 @@
                     to_relay(i).wait_recv()
                     to_onward(i).start()
 
-        tile(F1, c, OWN, 1)
+        tile(OWN, F1, c, 1)
 
         @pl.when(me.one)
         def _():
-            tile(F1, c, SIB, 2)
-
-    eig_ahead.wait_recv()
-
-    @pl.when(sib.cross)
-    def _():
-        eig_g.start()
+            tile(SIB, F1, c, 2)
 
     @pl.when(me.cross)
     def _():
@@ -220,7 +210,7 @@
 
         @pl.loop(0, chunks)
         def _(c):
-            tile(F1, c, G, 3)
+            tile(G, F1, c, 3)
 
     owners = {OWN: me, F1: Place(me.behind, count), G: side, F2: Place(me.far, count), SIB: sib}
     held = {OWN: None, F1: None, G: me.cross, F2: me.two, SIB: me.uses_sib}
@@ -257,6 +247,10 @@
                 out, _, when = part(slot, kind)
                 given(when, lambda: out().start())
 
+    @pl.when(me.two)
+    def _():
+        eig_ahead.start()
+
     send_parts(F1)
     send_parts(G)
     send_parts(SIB)
@@ -267,10 +261,18 @@
         def _(i):
             c = i // 2 + lax.rem(i, 2) * half
             to_far(c).wait_recv()
-            tile(F2, c, OWN, 2)
+            tile(OWN, F2, c, 2)
 
     send_parts(OWN)
     send_parts(F2)
+
+    @pl.when(me.one)
+    def _():
+        for c in range(half):
+            to_far(c).wait_send()
+        eig_far.start()
+        eig_ahead.start()
+
 
     def scale(slot):
         for kind in kinds:
@@ -304,9 +306,14 @@
 
     @pl.when(me.two)
     def _():
-        give(F2, by_rows(OWN, 2))
-
-    yacc[F1] = by_rows(OWN, 1)
+        give(F2, by_columns(OWN, 2))
+
+    yacc[F1] = by_columns(OWN, 1)
+    eig_ahead.wait_recv()
+
+    @pl.when(sib.cross)
+    def _():
+        eig_g.start()
 
     @pl.when(me.uses_sib)
     def _():
@@ -315,20 +322,20 @@
 
         @pl.when(me.one)
         def _():
-            yacc[F1] += by_rows(SIB, 2)
+            yacc[F1] += by_columns(SIB, 2)
 
     @pl.when(me.cross)
     def _():
         eig_g.wait_recv()
         scale(G)
-        yacc[F1] += by_rows(G, 3)
+        yacc[F1] += by_columns(G, 3)
 
     give(F1, yacc[F1])
     scale(F1)
 
     @pl.when(me.cross)
     def _():
-        give(G, by_columns(F1, 3))
+        give(G, by_rows(F1, 3))
 
     @pl.when(me.uses_sib)
     def _():
@@ -336,7 +343,7 @@
 
         @pl.when(me.one)
         def _():
-            yacc[SIB] += by_columns(F1, 2)
+            yacc[SIB] += by_rows(F1, 2)
 
         @pl.when(me.pair)
         def _():
@@ -345,13 +352,13 @@
         give(SIB, yacc[SIB])
 
     yacc[OWN] = by_columns(OWN, 0)
-    yacc[OWN] += by_columns(F1, 1)
+    yacc[OWN] += by_rows(F1, 1)
 
     @pl.when(me.two)
     def _():
         eig_far.wait_recv()
         scale(F2)
-        yacc[OWN] += by_columns(F2, 2)
+        yacc[OWN] += by_rows(F2, 2)
 
     @pl.when(me.pair)
     def _():
@@ -377,11 +384,6 @@
     def _():
         for c in range(chunks):
             to_g(c).wait_send()
-
-    @pl.when(me.one)
-    def _():
-        for c in range(half):
-            to_far(c).wait_send()
 
     @pl.when(me.one)
     def _():
@@ -422,7 +424,7 @@
             pltpu.VMEM((5, tiles, width), BF16),
             pltpu.VMEM((tiles // 2, width), BF16),
             pltpu.VMEM((4, tiles, tiles), BF16),
-            pltpu.VMEM((5, 1, tiles), F32),
+            pltpu.VMEM((5, tiles, 128), F32),
             pltpu.VMEM((5, 1, tiles), F32),
             pltpu.VMEM((5, 1, tiles), F32),
             pltpu.VMEM((5, 5, 1, tiles), F32),

time: 61 us -> 57.1 us (0.936)
  Pallas kernels: 59.2 us -> 55.3 us
    pallas_call x1, Pallas kernels: 59.2 us -> 55.3 us  [shards(): pl.pallas_call(functools.partial(kernel, count), out_shape=jax.ShapeDtype...]
where the time goes in v5:
time: 57.1 us; the launch traced here: 57 us
  Pallas kernels  55.3 us (97%)
  local copies, waits for them, and re-layouts  1.67 us (3%)
    pallas_call x1, Pallas kernels, shards(): pl.pallas_call(functools.partial(kernel, count), out_shape=jax.ShapeDtype...  55.3 us
    unnamed x1, local copies, waits for them, and re-layouts  1.67 us

profile of v5, /device:TPU:1, one launch (start us, length us, event | category | flops | bytes accessed | tf_op | source)
XLA Modules:
  0.0 57.0 jit_solution(7671317292578804333)
XLA Ops:
  0.0 55.3 %cluster.1 = f32[64,1024]{1,0:T(8,128)} custom-call(bf16[1024,768]{1,0:T(8,128)(2,1)} %x_hbm.1, bf16[64,1024]{1,0:T(8,128)(2,1)} %bitcast.3), custom_call_target="tpu_custom_call" | custom-call | tf_op jit(solution)/shard_map/cluster/pallas_call | solution.py:417
  55.3 1.7 %copy.4 = f32[1024,64]{0,1:T(8,128)} copy(f32[1024,64]{0,1:T(8,128)} %bitcast.2) | data formatting | bytes 524288

commit v6 on v5

--- a/solution.py
+++ b/solution.py
@@ -12,6 +12,7 @@
 MESH = pl.DeviceIdType.MESH
 OWN, SIB, F1, F2, G = range(5)
 CR = 256
+CROSSING = 2
 DIMS = (4, 4, 8)
 F32, BF16 = jnp.float32, jnp.bfloat16
 
@@ -47,15 +48,16 @@
         x, y, z = chip // (DIMS[1] * DIMS[2]), lax.rem(chip // DIMS[2], DIMS[1]), lax.rem(chip, DIMS[2])
         turn = jnp.where(first, z == DIMS[2] - 1, z == 0)
         across = dev + (DIMS[0] - 1 - 2 * x) * (2 * DIMS[1] * DIMS[2])
-        self.relay = jnp.where(turn, wrap(dev - s * 2 * DIMS[2]), across)
-        self.source = jnp.where(turn, wrap(dev + s * 2 * DIMS[2]), across)
+        column = lambda step: dev + (lax.rem(y + DIMS[1] + step, DIMS[1]) - y) * (2 * DIMS[2])
+        self.relay = jnp.where(turn, column(-s), across)
+        self.source = jnp.where(turn, column(s), across)
+        self.direct = jnp.where(jnp.logical_not(first) & (z == 0) & (y == 0), CROSSING, 2)
 
 
 def kernel(count, x_hbm, e_hbm, o_ref, raw, blk, rel, kst, bl, dacc, total, drecv, ebuf, sbuf, ymsg, yrecv, yacc,
            load_sem, sib_s, sib_r, f1_s, f1_r, f2_s, f2_r, g_s, g_r, rel_s, rel_r, e_s, e_r, y_s, y_r, d_s, d_r):
     tiles, width = raw.shape
     chunks = tiles // CR
-    half = chunks // 2
     a = math.sqrt(2.0 * width) / width * math.log2(math.e)
     me = Place(lax.axis_index("dev"), count)
     sib = Place(me.sib, count)
@@ -69,7 +71,8 @@
     partners = [me.sib, me.side, me.ahead, me.behind, me.far]
     source = Place(me.source, count)
     onward = source.far
-    partners += [me.relay, me.source, onward, Place(me.far, count).relay]
+    far = Place(me.far, count)
+    partners += [me.relay, me.source, onward, far.relay]
     barrier = pltpu.get_barrier_semaphore()
     for partner in partners:
         pl.semaphore_signal(barrier, inc=1, device_id=(partner,), device_id_type=MESH)
@@ -90,10 +93,10 @@
         return remote(blk.at[OWN, rows(c)], blk.at[F2, rows(c)], f2_s.at[c], f2_r.at[c], me.far)
 
     def to_relay(c):
-        return remote(blk.at[OWN, rows(c)], rel.at[rows(c - half)], rel_s.at[c - half], rel_r.at[c - half], me.relay)
+        return remote(blk.at[OWN, rows(c)], rel.at[rows(c)], rel_s.at[c], rel_r.at[c], me.relay)
 
     def to_onward(c):
-        return remote(rel.at[rows(c - half)], blk.at[F2, rows(c)], f2_s.at[c], f2_r.at[c], onward)
+        return remote(rel.at[rows(c)], blk.at[F2, rows(c)], f2_s.at[c], f2_r.at[c], onward)
 
     def to_g(c):
         return remote(blk.at[F1, rows(c)], blk.at[G, rows(c)], g_s.at[c], g_r.at[c], me.sib)
@@ -142,8 +145,8 @@
     pl.semaphore_wait(barrier, len(partners))
     for c in range(chunks):
         to_ahead(c).start()
-        if c >= half:
-            @pl.when(me.one)
+        if c > 0:
+            @pl.when(me.one & (c >= me.direct))
             def _():
                 to_relay(c).start()
         to_sib(c).start()
@@ -181,20 +184,18 @@
         def _():
             to_g(c).start()
 
-        @pl.when(c == chunks - 2)
-        def _():
-            @pl.when(me.one)
-            def _():
-                @pl.loop(0, half)
-                def _(i):
-                    to_far(i).start()
-
-            @pl.when(source.one)
-            def _():
-                @pl.loop(half, chunks)
-                def _(i):
-                    to_relay(i).wait_recv()
-                    to_onward(i).start()
+        @pl.when((c == chunks - 2) & me.one)
+        def _():
+            @pl.loop(0, me.direct)
+            def _(i):
+                to_far(i).start()
+
+        @pl.when((c == chunks - 2) & source.one)
+        def _():
+            @pl.loop(source.direct, chunks)
+            def _(i):
+                to_relay(i).wait_recv()
+                to_onward(i).start()
 
         tile(OWN, F1, c, 1)
 
@@ -212,7 +213,7 @@
         def _(c):
             tile(G, F1, c, 3)
 
-    owners = {OWN: me, F1: Place(me.behind, count), G: side, F2: Place(me.far, count), SIB: sib}
+    owners = {OWN: me, F1: Place(me.behind, count), G: side, F2: far, SIB: sib}
     held = {OWN: None, F1: None, G: me.cross, F2: me.two, SIB: me.uses_sib}
 
     def member(owner, kind):
@@ -259,7 +260,7 @@
     def _():
         @pl.loop(0, chunks)
         def _(i):
-            c = i // 2 + lax.rem(i, 2) * half
+            c = jnp.where(i == chunks - 1, i, lax.rem(jnp.where(far.direct == 1, i + 1, 2 * i), 3))
             to_far(c).wait_recv()
             tile(OWN, F2, c, 2)
 
@@ -268,8 +269,10 @@
 
     @pl.when(me.one)
     def _():
-        for c in range(half):
+        @pl.loop(0, me.direct)
+        def _(c):
             to_far(c).wait_send()
+
         eig_far.start()
         eig_ahead.start()
 
@@ -387,12 +390,14 @@
 
     @pl.when(me.one)
     def _():
-        for c in range(half, chunks):
+        @pl.loop(me.direct, chunks)
+        def _(c):
             to_relay(c).wait_send()
 
     @pl.when(source.one)
     def _():
-        for c in range(half, chunks):
+        @pl.loop(source.direct, chunks)
+        def _(c):
             to_onward(c).wait_send()
 
     eig_ahead.wait_send()
@@ -422,7 +427,7 @@
         scratch_shapes=[
             pltpu.VMEM((tiles, width), BF16),
             pltpu.VMEM((5, tiles, width), BF16),
-            pltpu.VMEM((tiles // 2, width), BF16),
+            pltpu.VMEM((tiles, width), BF16),
             pltpu.VMEM((4, tiles, tiles), BF16),
             pltpu.VMEM((5, tiles, 128), F32),
             pltpu.VMEM((5, 1, tiles), F32),

time: 57.1 us -> 57.1 us (level)
  no operation moved by 1% of the time
where the time goes in v6:
time: 57.1 us; the launch traced here: 57 us
  Pallas kernels  55.3 us (97%)
  local copies, waits for them, and re-layouts  1.67 us (3%)
    pallas_call x1, Pallas kernels, shards(): pl.pallas_call(functools.partial(kernel, count), out_shape=jax.ShapeDtype...  55.3 us
    unnamed x1, local copies, waits for them, and re-layouts  1.67 us

profile of v6, /device:TPU:1, one launch (start us, length us, event | category | flops | bytes accessed | tf_op | source)
XLA Modules:
  0.0 57.0 jit_solution(12425868333301164026)
XLA Ops:
  0.0 55.3 %cluster.1 = f32[64,1024]{1,0:T(8,128)} custom-call(bf16[1024,768]{1,0:T(8,128)(2,1)} %x_hbm.1, bf16[64,1024]{1,0:T(8,128)(2,1)} %bitcast.3), custom_call_target="tpu_custom_call" | custom-call | tf_op jit(solution)/shard_map/cluster/pallas_call | solution.py:422
  55.3 1.7 %copy.4 = f32[1024,64]{0,1:T(8,128)} copy(f32[1024,64]{0,1:T(8,128)} %bitcast.2) | data formatting | bytes 524288
